TPU v7x, 32 devices: a whole 2x2x4 slice. The times are simulated.
32 devices in a mesh: row: 4 (over x, core), col: 8 (over z, y).
Axes of the slice: x: 2, y: 2, z: 4, core: 2. Of those that a mesh axis runs over, the one named last changes fastest.
Arguments:
- density: float32 [2048, 2048], P('row', 'col'), may hold values from -0.4375 to 0.4375
- occupancy: int32 [16, 16], P('row', 'col'), may hold values from 0 to 1, as said below
Outputs:
- purified: float32 [2048, 2048], P('row', 'col')
Inputs may be any that keep to these rules, and one draw needn't show every extreme that they name: `occupancy`: 1 marks an occupied 128 x 128 tile, 0 an empty one; every diagonal tile is occupied.
All inputs are finite; a program needn't handle non-finite values.
Results may differ from a plain program's by a relative error of at most 0.0001.
Values sent between devices are 32-bit elements; how exact they have to be, the bound alone decides.
A program may use at most 64 MiB of HBM per device.

v0:
```python
import jax
import jax.numpy as jnp
from jax import lax
from jax.sharding import PartitionSpec as P

SECTIONS = 3


def from_root(block, axis, owner):
    block = jnp.where(lax.axis_index(axis) == owner, block, jnp.zeros_like(block))
    return lax.psum(block, axis)


def passed_along(value, axis, by):
    size = lax.axis_size(axis)
    return lax.ppermute(value, axis, [(i, (i + by) % size) for i in range(size)])


def tile_mask(values, occupancy):
    row_total, col_total = values.shape
    tile_rows, tile_cols = occupancy.shape
    shaped = values.reshape(tile_rows, row_total // tile_rows, tile_cols, col_total // tile_cols)
    weights = occupancy.astype(jnp.float32)[:, None, :, None]
    return (shaped * weights).reshape(row_total, col_total)


def left_blocks(masked):
    row_count = lax.axis_size("row")
    row_index = lax.axis_index("row")
    left_list = []
    for section_index in range(SECTIONS):
        owner_block = (row_index + section_index) % row_count
        halves = []
        for half_index in range(2):
            halves.append(from_root(masked, "col", 2 * owner_block + half_index))
        left_list.append(jnp.concatenate(halves, axis=1))
    return left_list


def right_rows(factor):
    right_list = [factor]
    current = factor
    for section_index in range(1, SECTIONS):
        current = passed_along(current, "row", -1)
        right_list.append(current)
    return right_list


def windowed(left_list, right_list):
    accum = jnp.zeros((left_list[0].shape[0], right_list[0].shape[1]), jnp.float32)
    for section_index in range(SECTIONS):
        accum = accum + jnp.dot(
            left_list[section_index],
            right_list[section_index],
            precision=lax.Precision.HIGHEST,
            preferred_element_type=jnp.float32,
        )
    return accum


def per_device(density, occupancy):
    masked = tile_mask(density, occupancy)
    left_list = left_blocks(masked)
    square_term = tile_mask(windowed(left_list, right_rows(masked)), occupancy)
    cube_term = tile_mask(windowed(left_list, right_rows(square_term)), occupancy)
    return 3.0 * square_term - 2.0 * cube_term


def solution(mesh):
    in_specs = (P("row", "col"), P("row", "col"))
    out_specs = P("row", "col")
    return jax.shard_map(
        per_device, mesh=mesh, in_specs=in_specs, out_specs=out_specs, check_vma=False
    )
```

profile of v0, /device:TPU:1, one launch (start us, length us, event | category | flops | bytes accessed | tf_op | source)
XLA Modules:
  0.0 178.7 jit_solution(14719848656112515283)
XLA Ops:
  6.5 0.7 convert_element_type.2
  7.3 0.1 copy.3
  7.4 0.2 mul.50
  7.6 0.0 copy-done
  7.6 0.9 broadcast_select_fusion
  8.5 1.6 broadcast_select_fusion.1
  10.1 0.0 all-reduce.3.cloned.1.call-update
  10.1 0.1 collective-permute-start
  10.2 9.4 %collective-permute-done = f32[512,256]{1,0:T(8,128)S(1)} collective-permute-done((f32[512,256]{1,0:T(8,128)S(1)}, f32[512,256]{1,0:T(8,128)S(1)}, u32[]{:S(2)}, u32[]{:S(2)}) %collective-permute-start) | collective-permute-done | bytes 524320 | tf_op jit(solution)/shard_map/ppermute | solution.py:16
  19.6 0.0 collective-permute-start.1
  19.6 125.5 %all-reduce.3.cloned.1.call-done = (f32[512,256]{1,0:T(8,128)}, f32[512,256]{1,0:T(8,128)}, f32[512,256]{1,0:T(8,128)}, f32[512,256]{1,0:T(8,128)}, f32[512,256]{1,0:T(8,128)}, /*index=5*/f32[512,256]{1,0:T(8,128)}) async-done(((f32[512,256]{1,0:T(8,128)}, f32[512,256]{1,0:T(8,128)}, f32[512,256]{1,0:T(8,128)}, f32[512,256]{1,0:T(8,128)}, f32[512,256]{1,0:T(8,128)}, /*index=5*/f32[512,256]{1,0:T(8,128)}), ...) | async-done | bytes 3145744 | tf_op jit(solution)/shard_map/psum | solution.py:11
  145.1 1.2 constant_dynamic-update-slice_fusion.5
  146.3 0.0 copy-done.3
  146.3 0.1 constant_dynamic-update-slice_fusion.1
  146.4 1.0 copy-done.2
  147.4 0.1 constant_dynamic-update-slice_fusion.3
  147.4 1.0 copy-done.1
  148.4 0.1 constant_dynamic-update-slice_fusion.4
  148.5 1.0 copy-done.4
  149.4 0.2 copy-done.5
  149.6 0.1 constant_dynamic-update-slice_fusion
  149.7 1.0 fusion.3
  150.7 1.0 convolution_add_fusion.3
  151.7 0.0 collective-permute-done.1
  151.8 1.0 fusion
  152.7 0.7 collective-permute-start.2
  153.5 7.9 %collective-permute-done.2 = f32[512,256]{1,0:T(8,128)S(1)} collective-permute-done((f32[512,256]{1,0:T(8,128)S(1)}, f32[512,256]{1,0:T(8,128)S(1)}, u32[]{:S(2)}, u32[]{:S(2)}) %collective-permute-start.2) | collective-permute-done | bytes 524320 | tf_op jit(solution)/shard_map/ppermute | solution.py:16
  161.4 0.0 collective-permute-start.3
  161.4 1.0 fusion.4
  162.4 1.0 convolution_add_fusion.1
  163.4 6.6 %collective-permute-done.3 = f32[512,256]{1,0:T(8,128)S(1)} collective-permute-done((f32[512,256]{1,0:T(8,128)S(1)}, f32[512,256]{1,0:T(8,128)S(1)}, u32[]{:S(2)}, u32[]{:S(2)}) %collective-permute-start.3) | collective-permute-done | bytes 524320 | tf_op jit(solution)/shard_map/ppermute | solution.py:16
  170.0 1.8 %multiply_subtract_fusion = f32[512,256]{1,0:T(8,128)} fusion(f32[512,256]{1,0:T(8,128)S(1)} %fusion, f32[64,8,2,128]{3,2,1,0:T(2,128)S(1)} %bitcast.23, f32[512,256]{1,0:T(8,128)S(1)} %convolution_add_fusion.1, f32[512,512]{1,0:T(8,128)S(1)} %constant_dynamic-update-slice_fusion.4, f32[512,256]{1,0:T(8,128)S(1)} %collective-permute-done.3), kind=kOutput, calls=%fused_computation.8 | convolution fusion | flops 805961728 | bytes 3670016 | tf_op jit(solution)/shard_map/dot_general | solution.py:52
  (7 shorter events, 0.0 us)
Async XLA Ops:
  6.5 1.1 copy-start
  6.5 138.6 %all-reduce.3.cloned.1.call-start = ((), (), s32[]{:S(2)}) async-start(), calls=%async_computation | async-start | bytes 6291456 | tf_op jit(solution)/shard_map/psum | solution.py:11
  10.1 9.5 %collective-permute-start = (f32[512,256]{1,0:T(8,128)S(1)}, f32[512,256]{1,0:T(8,128)S(1)}, u32[]{:S(2)}, u32[]{:S(2)}) collective-permute-start(f32[512,256]{1,0:T(8,128)S(1)} %get-tuple-element.12), channel_id=1, source_target_pairs={{0,24},{8,0},{16,8},{24,16},{1,25},{9,1},{17,9},{25,17},{2,26},{10... | collective-permute-start | bytes 1572872 | tf_op jit(solution)/shard_map/ppermute | solution.py:16
  19.6 132.1 %collective-permute-start.1 = (f32[512,256]{1,0:T(8,128)S(1)}, f32[512,256]{1,0:T(8,128)S(1)}, u32[]{:S(2)}, u32[]{:S(2)}) collective-permute-start(f32[512,256]{1,0:T(8,128)S(1)} %collective-permute-done), channel_id=1, source_target_pairs={{0,24},{8,0},{16,8},{24,16},{1,25},{9,1},{17,9},{25,17},{2,26},{10... | collective-permute-start | bytes 1572872 | tf_op jit(solution)/shard_map/ppermute | solution.py:16
  145.1 1.2 copy-start.3
  146.3 1.0 copy-start.2
  147.3 1.0 copy-start.1
  148.4 1.0 copy-start.4
  148.4 1.2 copy-start.5
  152.7 8.7 %collective-permute-start.2 = (f32[512,256]{1,0:T(8,128)S(1)}, f32[512,256]{1,0:T(8,128)S(1)}, u32[]{:S(2)}, u32[]{:S(2)}) collective-permute-start(f32[512,256]{1,0:T(8,128)S(1)} %fusion), channel_id=1, source_target_pairs={{0,24},{8,0},{16,8},{24,16},{1,25},{9,1},{17,9},{25,17},{2,26},{10... | collective-permute-start | bytes 1572872 | tf_op jit(solution)/shard_map/ppermute | solution.py:16
  161.4 8.6 %collective-permute-start.3 = (f32[512,256]{1,0:T(8,128)S(1)}, f32[512,256]{1,0:T(8,128)S(1)}, u32[]{:S(2)}, u32[]{:S(2)}) collective-permute-start(f32[512,256]{1,0:T(8,128)S(1)} %collective-permute-done.2), channel_id=1, source_target_pairs={{0,24},{8,0},{16,8},{24,16},{1,25},{9,1},{17,9},{25,17},{2,26},{10... | collective-permute-start | bytes 1572872 | tf_op jit(solution)/shard_map/ppermute | solution.py:16
Sparse Core Ops, SparseCore 0:
  11.6 133.5 all-reduce.2
where the time goes:
time: 179 us
  waiting for transfers between devices  149 us (83%)
  between operations  13.5 us (8%)
  matrix products  6.74 us (4%)
  local copies, waits for them, and re-layouts  4.9 us (3%)
  other arithmetic  3.2 us (2%)
    psum x1, waiting for transfers between devices, from_root(): return lax.psum(block, axis)  125 us
    ppermute x4, waiting for transfers between devices, passed_along(): lax.ppermute(value, axis, [(i, (i + by) % size) for i in range(size)])  24 us
    dot_general x6, matrix products, windowed(): jnp.dot(left_list[section_index], right_list[section_index], precision=la...  6.74 us
    unnamed x15, local copies, waits for them, and re-layouts  4.4 us
  transfers between devices with their start and end apart: 5, of which 4 were waited for; matrix products, arithmetic and copies ran while one was open for 3% of the time, Pallas kernels for 0%

commit v1 on v0

v1 whole, which is shorter than its diff:
```python
import functools

import jax
import jax.numpy as jnp
from jax import lax
from jax.experimental import pallas as pl
from jax.experimental.pallas import tpu as pltpu
from jax.sharding import PartitionSpec as P

SECTIONS = 3
CHUNKS = 4
ROW_TILE = 128
MESH = pl.DeviceIdType.MESH


def split(values):
    high = values.astype(jnp.bfloat16)
    low = (values - high.astype(jnp.float32)).astype(jnp.bfloat16)
    return high, low


def product(left_high, left_low, right_high, right_low):
    dot = functools.partial(jnp.dot, preferred_element_type=jnp.float32)
    return dot(left_high, right_high) + (dot(left_high, right_low) + dot(left_low, right_high))


def kernel(
    row_count, col_count, occ_ref, den_ref, out_ref,
    left, left_high, left_low, right, square, right_high, right_low, cube,
    left_recv, z_send, y_send, right_recv, right_send, square_recv, square_send,
):
    blk, half_cols = den_ref.shape
    rows = blk // CHUNKS
    tile_rows, tile_cols = occ_ref.shape
    tr, tc = blk // tile_rows, half_cols // tile_cols
    block_count = col_count // 2

    r, c = lax.axis_index("row"), lax.axis_index("col")
    place, half = lax.div(c, 2), lax.rem(c, 2)
    other = 1 - half
    core = lax.rem(r, 2)
    partner = c + 1 - 2 * half
    buddy = r + 1 - 2 * core
    above = lax.rem(r + row_count - 2, row_count)
    below = lax.rem(r + 2, row_count)
    has_prev, has_next = place > 0, place < block_count - 1
    own_section = lax.rem(place - r + block_count, block_count)

    barrier = pltpu.get_barrier_semaphore()

    def greet(**device):
        pl.semaphore_signal(barrier, inc=1, device_id=device, device_id_type=MESH)

    @pl.when(has_prev)
    def _():
        greet(col=c - 2)

    @pl.when(has_next)
    def _():
        greet(col=c + 2)

    greet(col=partner)
    greet(row=buddy)
    greet(row=above)
    if row_count > 4:
        greet(row=below)

    def masked_by_tiles(values, first_tile_row, count):
        lines = []
        for i in range(count):
            line = []
            for k in range(tile_cols):
                weight = occ_ref[first_tile_row + i, k].astype(jnp.float32)
                line.append(values[i * tr : (i + 1) * tr, k * tc : (k + 1) * tc] * weight)
            lines.append(jnp.concatenate(line, axis=1))
        return jnp.concatenate(lines, axis=0)

    for i in range(tile_rows):
        part = masked_by_tiles(den_ref[i * tr : (i + 1) * tr, :], i, 1)
        right[0, i * tr : (i + 1) * tr, :] = part

        @pl.when(own_section < SECTIONS)
        def _():
            left[own_section, half, i * tr : (i + 1) * tr, :] = part

    pl.semaphore_wait(
        barrier,
        has_prev.astype(jnp.int32) + has_next.astype(jnp.int32) + (4 if row_count > 4 else 3),
    )

    def left_copy(section, side, chunk, send_sem, **device):
        piece = left.at[section, side, pl.ds(chunk * rows, rows), :]
        return pltpu.make_async_remote_copy(
            src_ref=piece, dst_ref=piece, send_sem=send_sem,
            recv_sem=left_recv.at[section, side, chunk],
            device_id=device, device_id_type=MESH,
        )

    def spread(section, chunk, to_prev, to_next):
        if to_prev:
            @pl.when(has_prev)
            def _():
                left_copy(section, half, chunk, z_send.at[0, section], col=c - 2).start()

        if to_next:
            @pl.when(has_next)
            def _():
                left_copy(section, half, chunk, z_send.at[1, section], col=c + 2).start()

        left_copy(section, half, chunk, y_send.at[section], col=partner).start()

    def wait_left(section, side, chunk):
        left_copy(section, side, chunk, y_send.at[section], col=partner).wait_recv()

    def send_own(chunk):
        @pl.when(own_section < SECTIONS)
        def _():
            spread(own_section, chunk, True, True)

    def forward(chunk):
        if chunk + 1 < CHUNKS:
            send_own(chunk + 1)

        def step(distance, carry):
            for sign in (-1, 1):
                source = place + sign * distance
                section = lax.rem(source - r + 2 * block_count, block_count)
                inside = source >= 0 if sign < 0 else source < block_count

                @pl.when(jnp.logical_and(inside, section < SECTIONS))
                def _():
                    wait_left(section, half, chunk)
                    spread(section, chunk, sign > 0, sign < 0)

            return carry

        lax.fori_loop(1, block_count, step, 0)

    def right_copy(buffer, from_slot, to_slot, chunk, send_sem, recv_sems, device_row):
        span = pl.ds(chunk * rows, rows)
        return pltpu.make_async_remote_copy(
            src_ref=buffer.at[from_slot, span, :], dst_ref=buffer.at[to_slot, span, :],
            send_sem=send_sem, recv_sem=recv_sems.at[to_slot - 1, chunk],
            device_id={"row": device_row}, device_id_type=MESH,
        )

    def send_right(buffer, chunk, send_sems, recv_sems):
        right_copy(buffer, 0, 2, chunk, send_sems.at[0], recv_sems, above).start()

        @pl.when(core == 1)
        def _():
            right_copy(buffer, 0, 1, chunk, send_sems.at[1], recv_sems, buddy).start()

    def relay_right(buffer, chunk, send_sems, recv_sems):
        right_copy(buffer, 0, 2, chunk, send_sems.at[0], recv_sems, above).wait_recv()

        @pl.when(core == 0)
        def _():
            right_copy(buffer, 2, 1, chunk, send_sems.at[1], recv_sems, buddy).start()

    def wait_next(buffer, chunk, send_sems, recv_sems):
        right_copy(buffer, 0, 1, chunk, send_sems.at[1], recv_sems, buddy).wait_recv()

    def split_right(buffer, slot, first, count):
        high, low = split(buffer[slot, first : first + count, :])
        right_high[slot, first : first + count, :] = high
        right_low[slot, first : first + count, :] = low

    def consume(chunk):
        span = slice(chunk * rows, (chunk + 1) * rows)
        for section in range(SECTIONS):
            wait_left(section, other, chunk)
        total = jnp.zeros((rows, half_cols), jnp.float32)
        for section in range(SECTIONS):
            for side in range(2):
                high, low = split(left[section, side, span, :])
                left_high[section, side, span, :] = high
                left_low[section, side, span, :] = low
                depth = slice(side * half_cols, (side + 1) * half_cols)
                total = total + product(
                    high, low, right_high[section, depth, :], right_low[section, depth, :]
                )
        tiles = rows // tr
        square[0, span, :] = masked_by_tiles(total, chunk * tiles, tiles)
        send_right(square, chunk, square_send, square_recv)

    for chunk in range(CHUNKS):
        send_right(right, chunk, right_send, right_recv)
    send_own(0)

    for step in range(CHUNKS + 1):
        if step < CHUNKS:
            forward(step)
        if step == 1:
            for chunk in range(CHUNKS):
                relay_right(right, chunk, right_send, right_recv)
            split_right(right, 0, 0, blk)
            split_right(right, 2, 0, blk)
            for chunk in range(CHUNKS):
                wait_next(right, chunk, right_send, right_recv)
            split_right(right, 1, 0, blk)
        if step >= 1:
            consume(step - 1)
        if step >= 2:
            relay_right(square, step - 2, square_send, square_recv)

    def accumulate(terms, last):
        def step(tile, carry):
            span = pl.ds(pl.multiple_of(tile * ROW_TILE, ROW_TILE), ROW_TILE)
            total = cube[span, :] if last else jnp.zeros((ROW_TILE, half_cols), jnp.float32)
            for section, side in terms:
                depth = slice(side * half_cols, (side + 1) * half_cols)
                total = total + product(
                    left_high[section, side, span, :], left_low[section, side, span, :],
                    right_high[section, depth, :], right_low[section, depth, :],
                )
            cube[span, :] = total
            return carry

        lax.fori_loop(0, blk // ROW_TILE, step, 0)

    split_right(square, 0, 0, blk)
    for chunk in range(CHUNKS // 2):
        wait_next(square, chunk, square_send, square_recv)
    split_right(square, 1, 0, half_cols)
    split_right(square, 2, 0, half_cols)
    accumulate([(0, 0), (0, 1), (1, 0), (2, 0)], False)
    relay_right(square, CHUNKS - 1, square_send, square_recv)
    split_right(square, 2, half_cols, half_cols)
    for chunk in range(CHUNKS // 2, CHUNKS):
        wait_next(square, chunk, square_send, square_recv)
    split_right(square, 1, half_cols, half_cols)
    accumulate([(1, 1), (2, 1)], True)

    for i in range(tile_rows):
        span = slice(i * tr, (i + 1) * tr)
        out_ref[span, :] = 3.0 * square[0, span, :] - 2.0 * masked_by_tiles(cube[span, :], i, 1)

    def all_sent(whole, send_sem):
        pltpu.make_async_copy(whole, whole, send_sem).wait()

    for section in range(SECTIONS):
        source = lax.rem(r + section, block_count)
        whole = left.at[section, half]

        @pl.when(jnp.logical_and(has_prev, source >= place))
        def _():
            all_sent(whole, z_send.at[0, section])

        @pl.when(jnp.logical_and(has_next, source <= place))
        def _():
            all_sent(whole, z_send.at[1, section])

        all_sent(whole, y_send.at[section])
    for sems in (right_send, square_send):
        for k in range(2):
            all_sent(right.at[0], sems.at[k])


def per_device(density, occupancy):
    blk, half_cols = density.shape
    row_count, col_count = lax.axis_size("row"), lax.axis_size("col")
    dma = pltpu.SemaphoreType.DMA
    wide = (SECTIONS, 2, blk, half_cols)
    tall = (SECTIONS, blk, half_cols)
    flops = 12 * blk * SECTIONS * blk * half_cols
    return pl.pallas_call(
        functools.partial(kernel, row_count, col_count),
        out_shape=jax.ShapeDtypeStruct(density.shape, jnp.float32),
        in_specs=[
            pl.BlockSpec(memory_space=pltpu.SMEM),
            pl.BlockSpec(memory_space=pltpu.VMEM),
        ],
        out_specs=pl.BlockSpec(memory_space=pltpu.VMEM),
        scratch_shapes=[
            pltpu.VMEM(wide, jnp.float32),
            pltpu.VMEM(wide, jnp.bfloat16),
            pltpu.VMEM(wide, jnp.bfloat16),
            pltpu.VMEM(tall, jnp.float32),
            pltpu.VMEM(tall, jnp.float32),
            pltpu.VMEM(tall, jnp.bfloat16),
            pltpu.VMEM(tall, jnp.bfloat16),
            pltpu.VMEM((blk, half_cols), jnp.float32),
            dma((SECTIONS, 2, CHUNKS)),
            dma((2, SECTIONS)),
            dma((SECTIONS,)),
            dma((2, CHUNKS)),
            dma((2,)),
            dma((2, CHUNKS)),
            dma((2,)),
        ],
        compiler_params=pltpu.CompilerParams(
            collective_id=0, has_side_effects=True, vmem_limit_bytes=40 * 2**20
        ),
        cost_estimate=pl.CostEstimate(
            flops=flops, bytes_accessed=2 * 4 * blk * half_cols, transcendentals=0
        ),
    )(occupancy, density)


def solution(mesh):
    in_specs = (P("row", "col"), P("row", "col"))
    out_specs = P("row", "col")
    return jax.shard_map(
        per_device, mesh=mesh, in_specs=in_specs, out_specs=out_specs, check_vma=False
    )
```

time: 179 us -> 53.9 us (0.30)
  waiting for transfers between devices: 149 us -> 0 us
  Pallas kernels: 0 us -> 51.1 us
  between operations: 13.5 us -> 0.01 us
  matrix products: 6.74 us -> 0 us
  other arithmetic: 3.2 us -> 0 us
  local copies, waits for them, and re-layouts: 4.9 us -> 2.6 us
    psum x1 -> x0, waiting for transfers between devices: 125 us -> none  [from_root(): return lax.psum(block, axis)]
    pallas_call x0 -> x1, Pallas kernels: none -> 51.1 us  [per_device(): pl.pallas_call(functools.partial(kernel, row_count, col_count), out_shape...]
    ppermute x4 -> x0, waiting for transfers between devices: 24 us -> none  [passed_along(): lax.ppermute(value, axis, [(i, (i + by) % size) for i in range(size)])]
    dot_general x6 -> x0, matrix products: 6.74 us -> none  [windowed(): jnp.dot(left_list[section_index], right_list[section_index], precision=la...]
    select_n x2 -> x0, other arithmetic: 2.47 us -> none  [from_root(): jnp.where(lax.axis_index(axis) == owner, block, jnp.zeros_like(block))]
    unnamed x15 -> x4, local copies, waits for them, and re-layouts: 4.4 us -> 2.6 us
  transfers between devices with their start and end apart: 5 -> 0, of which waited for: 4 -> 0; matrix products, arithmetic and copies ran while one was open for 3% -> 0% of each run, Pallas kernels for 0% -> 0%
where the time goes in v1:
time: 53.9 us; the launch traced here: 53.7 us
  Pallas kernels  51.1 us (95%)
  local copies, waits for them, and re-layouts  2.6 us (5%)
    pallas_call x1, Pallas kernels, per_device(): pl.pallas_call(functools.partial(kernel, row_count, col_count), out_shape...  51.1 us
    unnamed x4, local copies, waits for them, and re-layouts  2.6 us

profile of v1, /device:TPU:1, one launch (start us, length us, event | category | flops | bytes accessed | tf_op | source)
XLA Modules:
  0.0 53.7 jit_solution(10340191811199741634)
XLA Ops:
  0.0 0.8 %copy.3.occ_ref = s32[4,2]{1,0:T(4,128)S(1)} copy(s32[4,2]{0,1:T(2,128)} %param.3) | data formatting | bytes 64 | tf_op args[1]
  0.8 0.0 copy-start
  0.8 1.0 %copy-done = f32[512,256]{1,0:T(8,128)S(1)} copy-done((f32[512,256]{1,0:T(8,128)S(1)}, f32[512,256]{1,0:T(8,128)}, u32[]{:S(2)}) %copy-start) | copy-done | bytes 524312
  1.8 51.1 %shard_map.28 = f32[512,256]{1,0:T(8,128)S(1)} custom-call(s32[4,2]{1,0:T(4,128)S(1)} %copy.3.occ_ref, f32[512,256]{1,0:T(8,128)S(1)} %copy-done), custom_call_target="tpu_custom_call" | custom-call | flops 2415919104 | bytes 1048576 | tf_op jit(solution)/shard_map/pallas_call | solution.py:267
  52.9 0.8 %copy.5 = f32[512,256]{1,0:T(8,128)} copy(f32[512,256]{1,0:T(8,128)S(1)} %shard_map.28) | data formatting | bytes 1048576
Async XLA Ops:
  0.8 1.0 %copy-start = (f32[512,256]{1,0:T(8,128)S(1)}, f32[512,256]{1,0:T(8,128)}, u32[]{:S(2)}) copy-start(f32[512,256]{1,0:T(8,128)} %den_ref.1) | copy-start | bytes 1572868

commit v2 on v1

--- a/solution.py
+++ b/solution.py
@@ -8,7 +8,7 @@
 from jax.sharding import PartitionSpec as P
 
 SECTIONS = 3
-CHUNKS = 4
+CHUNKS = 8
 ROW_TILE = 128
 MESH = pl.DeviceIdType.MESH
 
@@ -21,17 +21,19 @@
 
 def product(left_high, left_low, right_high, right_low):
     dot = functools.partial(jnp.dot, preferred_element_type=jnp.float32)
-    return dot(left_high, right_high) + (dot(left_high, right_low) + dot(left_low, right_high))
+    count = left_high.shape[0]
+    both = dot(jnp.concatenate([left_high, left_low], axis=0), right_high)
+    return both[:count] + (both[count:] + dot(left_high, right_low))
 
 
 def kernel(
     row_count, col_count, occ_ref, den_ref, out_ref,
     left, left_high, left_low, right, square, right_high, right_low, cube,
-    left_recv, z_send, y_send, right_recv, right_send, square_recv, square_send,
+    left_recv, z_send, y_send, right_recv, right_send, square_recv, square_send, load_sem,
 ):
     blk, half_cols = den_ref.shape
     rows = blk // CHUNKS
-    tile_rows, tile_cols = occ_ref.shape
+    tile_cols, tile_rows = occ_ref.shape
     tr, tc = blk // tile_rows, half_cols // tile_cols
     block_count = col_count // 2
 
@@ -46,6 +48,9 @@
     has_prev, has_next = place > 0, place < block_count - 1
     own_section = lax.rem(place - r + block_count, block_count)
 
+    load = pltpu.make_async_copy(den_ref, cube, load_sem)
+    load.start()
+
     barrier = pltpu.get_barrier_semaphore()
 
     def greet(**device):
@@ -65,18 +70,20 @@
     if row_count > 4:
         greet(row=below)
 
-    def masked_by_tiles(values, first_tile_row, count):
+    def masked_by_tiles(values, first_row):
+        count = min(tr, values.shape[0])
         lines = []
-        for i in range(count):
+        for i in range(0, values.shape[0], count):
             line = []
             for k in range(tile_cols):
-                weight = occ_ref[first_tile_row + i, k].astype(jnp.float32)
-                line.append(values[i * tr : (i + 1) * tr, k * tc : (k + 1) * tc] * weight)
+                weight = occ_ref[k, (first_row + i) // tr].astype(jnp.float32)
+                line.append(values[i : i + count, k * tc : (k + 1) * tc] * weight)
             lines.append(jnp.concatenate(line, axis=1))
         return jnp.concatenate(lines, axis=0)
 
+    load.wait()
     for i in range(tile_rows):
-        part = masked_by_tiles(den_ref[i * tr : (i + 1) * tr, :], i, 1)
+        part = masked_by_tiles(cube[i * tr : (i + 1) * tr, :], i * tr)
         right[0, i * tr : (i + 1) * tr, :] = part
 
         @pl.when(own_section < SECTIONS)
@@ -180,8 +187,7 @@
                 total = total + product(
                     high, low, right_high[section, depth, :], right_low[section, depth, :]
                 )
-        tiles = rows // tr
-        square[0, span, :] = masked_by_tiles(total, chunk * tiles, tiles)
+        square[0, span, :] = masked_by_tiles(total, chunk * rows)
         send_right(square, chunk, square_send, square_recv)
 
     for chunk in range(CHUNKS):
@@ -234,7 +240,7 @@
 
     for i in range(tile_rows):
         span = slice(i * tr, (i + 1) * tr)
-        out_ref[span, :] = 3.0 * square[0, span, :] - 2.0 * masked_by_tiles(cube[span, :], i, 1)
+        out_ref[span, :] = 3.0 * square[0, span, :] - 2.0 * masked_by_tiles(cube[span, :], i * tr)
 
     def all_sent(whole, send_sem):
         pltpu.make_async_copy(whole, whole, send_sem).wait()
@@ -269,7 +275,7 @@
         out_shape=jax.ShapeDtypeStruct(density.shape, jnp.float32),
         in_specs=[
             pl.BlockSpec(memory_space=pltpu.SMEM),
-            pl.BlockSpec(memory_space=pltpu.VMEM),
+            pl.BlockSpec(memory_space=pltpu.HBM),
         ],
         out_specs=pl.BlockSpec(memory_space=pltpu.VMEM),
         scratch_shapes=[
@@ -288,6 +294,7 @@
             dma((2,)),
             dma((2, CHUNKS)),
             dma((2,)),
+            dma,
         ],
         compiler_params=pltpu.CompilerParams(
             collective_id=0, has_side_effects=True, vmem_limit_bytes=40 * 2**20
@@ -295,7 +302,7 @@
         cost_estimate=pl.CostEstimate(
             flops=flops, bytes_accessed=2 * 4 * blk * half_cols, transcendentals=0
         ),
-    )(occupancy, density)
+    )(occupancy.T, density)
 
 
 def solution(mesh):

time: 53.9 us -> 64.6 us (1.20)
  Pallas kernels: 51.1 us -> 61.9 us
    pallas_call x1, Pallas kernels: 51.1 us -> 61.9 us  [per_device(): pl.pallas_call(functools.partial(kernel, row_count, col_count), out_shape...]
    unnamed x4 -> x5, local copies, waits for them, and re-layouts: 2.6 us -> 2.52 us
where the time goes in v2:
time: 64.6 us; the launch traced here: 64.4 us
  Pallas kernels  61.9 us (96%)
  local copies, waits for them, and re-layouts  2.52 us (4%)
    pallas_call x1, Pallas kernels, per_device(): pl.pallas_call(functools.partial(kernel, row_count, col_count), out_shape...  61.9 us
    unnamed x5, local copies, waits for them, and re-layouts  2.52 us

profile of v2, /device:TPU:1, one launch (start us, length us, event | category | flops | bytes accessed | tf_op | source)
XLA Modules:
  0.0 64.4 jit_solution(6324366697966140535)
XLA Ops:
  0.0 0.0 copy-start.1
  0.0 0.7 %copy-done.1 = s32[4,2]{0,1:T(2,128)S(1)} copy-done((s32[4,2]{0,1:T(2,128)S(1)}, s32[4,2]{0,1:T(2,128)}, u32[]{:S(2)}) %copy-start.1) | copy-done | bytes 56
  0.7 0.0 copy-start
  0.7 1.0 %copy-done = f32[512,256]{1,0:T(8,128)S(1)} copy-done((f32[512,256]{1,0:T(8,128)S(1)}, f32[512,256]{1,0:T(8,128)}, u32[]{:S(2)}) %copy-start) | copy-done | bytes 524312
  1.7 61.9 %shard_map.28 = f32[512,256]{1,0:T(8,128)S(1)} custom-call(s32[2,4]{1,0:T(2,128)S(1)} %bitcast.1, f32[512,256]{1,0:T(8,128)S(1)} %copy-done), custom_call_target="tpu_custom_call" | custom-call | flops 2415919104 | bytes 1048576 | tf_op jit(solution)/shard_map/pallas_call | solution.py:273
  63.6 0.8 %copy.4 = f32[512,256]{1,0:T(8,128)} copy(f32[512,256]{1,0:T(8,128)S(1)} %shard_map.28) | data formatting | bytes 1048576
Async XLA Ops:
  0.0 0.7 %copy-start.1 = (s32[4,2]{0,1:T(2,128)S(1)}, s32[4,2]{0,1:T(2,128)}, u32[]{:S(2)}) copy-start(s32[4,2]{0,1:T(2,128)} %param.3) | copy-start | bytes 100
  0.7 1.0 %copy-start = (f32[512,256]{1,0:T(8,128)S(1)}, f32[512,256]{1,0:T(8,128)}, u32[]{:S(2)}) copy-start(f32[512,256]{1,0:T(8,128)} %den_ref.1) | copy-start | bytes 1572868

commit v3 on v2

--- a/solution.py
+++ b/solution.py
@@ -9,6 +9,8 @@
 
 SECTIONS = 3
 CHUNKS = 8
+GROUPS = ((0, 2), (2, 2), (4, 2), (6, 1), (7, 1))
+AHEAD = 2
 ROW_TILE = 128
 MESH = pl.DeviceIdType.MESH
 
@@ -124,11 +126,12 @@
         def _():
             spread(own_section, chunk, True, True)
 
-    def forward(chunk):
-        if chunk + 1 < CHUNKS:
-            send_own(chunk + 1)
+    def forward(now):
+        if now + AHEAD < CHUNKS:
+            send_own(now + AHEAD)
 
         def step(distance, carry):
+            chunk = now + 1 - distance
             for sign in (-1, 1):
                 source = place + sign * distance
                 section = lax.rem(source - r + 2 * block_count, block_count)
@@ -141,7 +144,7 @@
 
             return carry
 
-        lax.fori_loop(1, block_count, step, 0)
+        lax.fori_loop(max(1, now + 2 - CHUNKS), min(block_count - 1, now + 1) + 1, step, 0)
 
     def right_copy(buffer, from_slot, to_slot, chunk, send_sem, recv_sems, device_row):
         span = pl.ds(chunk * rows, rows)
@@ -173,11 +176,12 @@
         right_high[slot, first : first + count, :] = high
         right_low[slot, first : first + count, :] = low
 
-    def consume(chunk):
-        span = slice(chunk * rows, (chunk + 1) * rows)
-        for section in range(SECTIONS):
-            wait_left(section, other, chunk)
-        total = jnp.zeros((rows, half_cols), jnp.float32)
+    def consume(first, count):
+        span = slice(first * rows, (first + count) * rows)
+        for chunk in range(first, first + count):
+            for section in range(SECTIONS):
+                wait_left(section, other, chunk)
+        total = jnp.zeros((count * rows, half_cols), jnp.float32)
         for section in range(SECTIONS):
             for side in range(2):
                 high, low = split(left[section, side, span, :])
@@ -187,17 +191,24 @@
                 total = total + product(
                     high, low, right_high[section, depth, :], right_low[section, depth, :]
                 )
-        square[0, span, :] = masked_by_tiles(total, chunk * rows)
-        send_right(square, chunk, square_send, square_recv)
+        square[0, span, :] = masked_by_tiles(total, first * rows)
+        for chunk in range(first, first + count):
+            send_right(square, chunk, square_send, square_recv)
 
     for chunk in range(CHUNKS):
         send_right(right, chunk, right_send, right_recv)
-    send_own(0)
-
-    for step in range(CHUNKS + 1):
-        if step < CHUNKS:
-            forward(step)
-        if step == 1:
+    for chunk in range(AHEAD):
+        send_own(chunk)
+
+    lag = block_count - 1
+    pending = None
+    for now in range(CHUNKS + lag):
+        if now < CHUNKS + lag - 1:
+            forward(now)
+        done = [g for g in GROUPS if g[0] + g[1] - 1 + lag == now]
+        if not done:
+            continue
+        if done[0][0] == 0:
             for chunk in range(CHUNKS):
                 relay_right(right, chunk, right_send, right_recv)
             split_right(right, 0, 0, blk)
@@ -205,10 +216,11 @@
             for chunk in range(CHUNKS):
                 wait_next(right, chunk, right_send, right_recv)
             split_right(right, 1, 0, blk)
-        if step >= 1:
-            consume(step - 1)
-        if step >= 2:
-            relay_right(square, step - 2, square_send, square_recv)
+        consume(*done[0])
+        if pending:
+            for chunk in range(pending[0], sum(pending)):
+                relay_right(square, chunk, square_send, square_recv)
+        pending = done[0]
 
     def accumulate(terms, last):
         def step(tile, carry):

time: 64.6 us -> 53.5 us (0.83)
  the two profiles are of different devices: /device:TPU:1 before, /device:TPU:25 now
where the time goes in v3:
time: 53.5 us; the launch traced here: 53.3 us
  Pallas kernels  50.8 us (95%)
  local copies, waits for them, and re-layouts  2.52 us (5%)
    pallas_call x1, Pallas kernels, per_device(): pl.pallas_call(functools.partial(kernel, row_count, col_count), out_shape...  50.8 us
    unnamed x5, local copies, waits for them, and re-layouts  2.52 us

profile of v3, /device:TPU:25, one launch (start us, length us, event | category | flops | bytes accessed | tf_op | source)
XLA Modules:
  0.0 53.3 jit_solution(2475254671621859266)
XLA Ops:
  0.0 0.0 copy-start.1
  0.0 0.7 %copy-done.1 = s32[4,2]{0,1:T(2,128)S(1)} copy-done((s32[4,2]{0,1:T(2,128)S(1)}, s32[4,2]{0,1:T(2,128)}, u32[]{:S(2)}) %copy-start.1) | copy-done | bytes 56
  0.7 0.0 copy-start
  0.7 1.0 %copy-done = f32[512,256]{1,0:T(8,128)S(1)} copy-done((f32[512,256]{1,0:T(8,128)S(1)}, f32[512,256]{1,0:T(8,128)}, u32[]{:S(2)}) %copy-start) | copy-done | bytes 524312
  1.7 50.8 %shard_map.28 = f32[512,256]{1,0:T(8,128)S(1)} custom-call(s32[2,4]{1,0:T(2,128)S(1)} %bitcast.1, f32[512,256]{1,0:T(8,128)S(1)} %copy-done), custom_call_target="tpu_custom_call" | custom-call | flops 2415919104 | bytes 1048576 | tf_op jit(solution)/shard_map/pallas_call | solution.py:285
  52.5 0.8 %copy.4 = f32[512,256]{1,0:T(8,128)} copy(f32[512,256]{1,0:T(8,128)S(1)} %shard_map.28) | data formatting | bytes 1048576
Async XLA Ops:
  0.0 0.7 %copy-start.1 = (s32[4,2]{0,1:T(2,128)S(1)}, s32[4,2]{0,1:T(2,128)}, u32[]{:S(2)}) copy-start(s32[4,2]{0,1:T(2,128)} %param.3) | copy-start | bytes 100
  0.7 1.0 %copy-start = (f32[512,256]{1,0:T(8,128)S(1)}, f32[512,256]{1,0:T(8,128)}, u32[]{:S(2)}) copy-start(f32[512,256]{1,0:T(8,128)} %den_ref.1) | copy-start | bytes 1572868

commit v4 on v3

--- a/solution.py
+++ b/solution.py
@@ -11,6 +11,7 @@
 CHUNKS = 8
 GROUPS = ((0, 2), (2, 2), (4, 2), (6, 1), (7, 1))
 AHEAD = 2
+ACROSS = 3
 ROW_TILE = 128
 MESH = pl.DeviceIdType.MESH
 
@@ -31,7 +32,7 @@
 def kernel(
     row_count, col_count, occ_ref, den_ref, out_ref,
     left, left_high, left_low, right, square, right_high, right_low, cube,
-    left_recv, z_send, y_send, right_recv, right_send, square_recv, square_send, load_sem,
+    left_recv, z_send, y_send, right_recv, right_send, square_recv, square_send, load_sem, across_send,
 ):
     blk, half_cols = den_ref.shape
     rows = blk // CHUNKS
@@ -116,7 +117,21 @@
             def _():
                 left_copy(section, half, chunk, z_send.at[1, section], col=c + 2).start()
 
-        left_copy(section, half, chunk, y_send.at[section], col=partner).start()
+        @pl.when(jnp.logical_or(section == own_section, chunk != ACROSS))
+        def _():
+            left_copy(section, half, chunk, y_send.at[section], col=partner).start()
+
+    def pass_across(section, to_prev, to_next):
+        wait_left(section, other, ACROSS)
+        if to_prev:
+            @pl.when(has_prev)
+            def _():
+                left_copy(section, other, ACROSS, across_send.at[0, section], col=c - 2).start()
+
+        if to_next:
+            @pl.when(has_next)
+            def _():
+                left_copy(section, other, ACROSS, across_send.at[1, section], col=c + 2).start()
 
     def wait_left(section, side, chunk):
         left_copy(section, side, chunk, y_send.at[section], col=partner).wait_recv()
@@ -144,7 +159,25 @@
 
             return carry
 
+        def step_across(distance):
+            if distance == 0:
+                @pl.when(own_section < SECTIONS)
+                def _():
+                    pass_across(own_section, True, True)
+
+                return
+            for sign in (-1, 1):
+                source = place + sign * distance
+                section = lax.rem(source - r + 2 * block_count, block_count)
+                inside = source >= 0 if sign < 0 else source < block_count
+
+                @pl.when(jnp.logical_and(inside, section < SECTIONS))
+                def _():
+                    pass_across(section, sign > 0, sign < 0)
+
         lax.fori_loop(max(1, now + 2 - CHUNKS), min(block_count - 1, now + 1) + 1, step, 0)
+        if 0 <= now - ACROSS < block_count:
+            step_across(now - ACROSS)
 
     def right_copy(buffer, from_slot, to_slot, chunk, send_sem, recv_sems, device_row):
         span = pl.ds(chunk * rows, rows)
@@ -179,7 +212,7 @@
     def consume(first, count):
         span = slice(first * rows, (first + count) * rows)
         for chunk in range(first, first + count):
-            for section in range(SECTIONS):
+            for section in range(SECTIONS if chunk != ACROSS else 0):
                 wait_left(section, other, chunk)
         total = jnp.zeros((count * rows, half_cols), jnp.float32)
         for section in range(SECTIONS):
@@ -260,16 +293,24 @@
     for section in range(SECTIONS):
         source = lax.rem(r + section, block_count)
         whole = left.at[section, half]
+        piece = left.at[section, other, pl.ds(0, rows), :]
 
         @pl.when(jnp.logical_and(has_prev, source >= place))
         def _():
             all_sent(whole, z_send.at[0, section])
+            all_sent(piece, across_send.at[0, section])
 
         @pl.when(jnp.logical_and(has_next, source <= place))
         def _():
             all_sent(whole, z_send.at[1, section])
-
-        all_sent(whole, y_send.at[section])
+            all_sent(piece, across_send.at[1, section])
+
+        all_sent(left.at[section, half, pl.ds(0, blk - rows), :], y_send.at[section])
+
+        @pl.when(source == place)
+        def _():
+            all_sent(piece, y_send.at[section])
+
     for sems in (right_send, square_send):
         for k in range(2):
             all_sent(right.at[0], sems.at[k])
@@ -307,9 +348,10 @@
             dma((2, CHUNKS)),
             dma((2,)),
             dma,
+            dma((2, SECTIONS)),
         ],
         compiler_params=pltpu.CompilerParams(
-            collective_id=0, has_side_effects=True, vmem_limit_bytes=40 * 2**20
+            collective_id=0, has_side_effects=True, vmem_limit_bytes=64 * 2**20 - 800 * 2**10
         ),
         cost_estimate=pl.CostEstimate(
             flops=flops, bytes_accessed=2 * 4 * blk * half_cols, transcendentals=0

time: 53.5 us -> 55.3 us (1.034)
  Pallas kernels: 50.8 us -> 53.2 us
  local copies, waits for them, and re-layouts: 2.52 us -> 1.87 us
    pallas_call x1, Pallas kernels: 50.8 us -> 53.2 us  [per_device(): pl.pallas_call(functools.partial(kernel, row_count, col_count), out_shape...]
    unnamed x5 -> x1, local copies, waits for them, and re-layouts: 2.52 us -> 1.87 us
where the time goes in v4:
time: 55.3 us; the launch traced here: 55.1 us
  Pallas kernels  53.2 us (96%)
  local copies, waits for them, and re-layouts  1.87 us (3%)
    pallas_call x1, Pallas kernels, per_device(): pl.pallas_call(functools.partial(kernel, row_count, col_count), out_shape...  53.2 us
    unnamed x1, local copies, waits for them, and re-layouts  1.87 us

profile of v4, /device:TPU:25, one launch (start us, length us, event | category | flops | bytes accessed | tf_op | source)
XLA Modules:
  0.0 55.1 jit_solution(8417378613892587122)
XLA Ops:
  0.0 53.2 %shard_map.28 = f32[512,256]{1,0:T(8,128)} custom-call(s32[2,4]{1,0:T(2,128)} %bitcast.1, f32[512,256]{1,0:T(8,128)} %den_ref.1), custom_call_target="tpu_custom_call" | custom-call | flops 2415919104 | bytes 1048576 | tf_op jit(solution)/shard_map/pallas_call | solution.py:326
  53.2 1.9 %copy.4 = f32[512,256]{1,0:T(8,128)} copy(f32[512,256]{1,0:T(8,128)} %shard_map.28) | data formatting | bytes 1048576

commit v5 on v3

--- a/solution.py
+++ b/solution.py
@@ -47,7 +47,6 @@
     buddy = r + 1 - 2 * core
     above = lax.rem(r + row_count - 2, row_count)
     below = lax.rem(r + 2, row_count)
-    has_prev, has_next = place > 0, place < block_count - 1
     own_section = lax.rem(place - r + block_count, block_count)
 
     load = pltpu.make_async_copy(den_ref, cube, load_sem)
@@ -58,14 +57,18 @@
     def greet(**device):
         pl.semaphore_signal(barrier, inc=1, device_id=device, device_id_type=MESH)
 
-    @pl.when(has_prev)
-    def _():
-        greet(col=c - 2)
-
-    @pl.when(has_next)
-    def _():
-        greet(col=c + 2)
-
+    def greet_line(distance, carry):
+        @pl.when(place >= distance)
+        def _():
+            greet(col=c - 2 * distance)
+
+        @pl.when(place + distance < block_count)
+        def _():
+            greet(col=c + 2 * distance)
+
+        return carry
+
+    lax.fori_loop(1, block_count, greet_line, 0)
     greet(col=partner)
     greet(row=buddy)
     greet(row=above)
@@ -92,10 +95,7 @@
         def _():
             left[own_section, half, i * tr : (i + 1) * tr, :] = part
 
-    pl.semaphore_wait(
-        barrier,
-        has_prev.astype(jnp.int32) + has_next.astype(jnp.int32) + (4 if row_count > 4 else 3),
-    )
+    pl.semaphore_wait(barrier, block_count - 1 + (4 if row_count > 4 else 3))
 
     def left_copy(section, side, chunk, send_sem, **device):
         piece = left.at[section, side, pl.ds(chunk * rows, rows), :]
@@ -105,17 +105,7 @@
             device_id=device, device_id_type=MESH,
         )
 
-    def spread(section, chunk, to_prev, to_next):
-        if to_prev:
-            @pl.when(has_prev)
-            def _():
-                left_copy(section, half, chunk, z_send.at[0, section], col=c - 2).start()
-
-        if to_next:
-            @pl.when(has_next)
-            def _():
-                left_copy(section, half, chunk, z_send.at[1, section], col=c + 2).start()
-
+    def to_partner(section, chunk):
         left_copy(section, half, chunk, y_send.at[section], col=partner).start()
 
     def wait_left(section, side, chunk):
@@ -124,27 +114,32 @@
     def send_own(chunk):
         @pl.when(own_section < SECTIONS)
         def _():
-            spread(own_section, chunk, True, True)
-
-    def forward(now):
-        if now + AHEAD < CHUNKS:
-            send_own(now + AHEAD)
-
-        def step(distance, carry):
-            chunk = now + 1 - distance
-            for sign in (-1, 1):
-                source = place + sign * distance
-                section = lax.rem(source - r + 2 * block_count, block_count)
-                inside = source >= 0 if sign < 0 else source < block_count
-
-                @pl.when(jnp.logical_and(inside, section < SECTIONS))
+            def step(distance, carry):
+                @pl.when(place >= distance)
                 def _():
-                    wait_left(section, half, chunk)
-                    spread(section, chunk, sign > 0, sign < 0)
-
-            return carry
-
-        lax.fori_loop(max(1, now + 2 - CHUNKS), min(block_count - 1, now + 1) + 1, step, 0)
+                    left_copy(
+                        own_section, half, chunk, z_send.at[0, distance - 1], col=c - 2 * distance
+                    ).start()
+
+                @pl.when(place + distance < block_count)
+                def _():
+                    left_copy(
+                        own_section, half, chunk, z_send.at[1, distance - 1], col=c + 2 * distance
+                    ).start()
+
+                return carry
+
+            to_partner(own_section, chunk)
+            lax.fori_loop(1, block_count, step, 0)
+
+    def forward(chunk):
+        if chunk + AHEAD < CHUNKS:
+            send_own(chunk + AHEAD)
+        for section in range(SECTIONS):
+            @pl.when(section != own_section)
+            def _():
+                wait_left(section, half, chunk)
+                to_partner(section, chunk)
 
     def right_copy(buffer, from_slot, to_slot, chunk, send_sem, recv_sems, device_row):
         span = pl.ds(chunk * rows, rows)
@@ -200,10 +195,10 @@
     for chunk in range(AHEAD):
         send_own(chunk)
 
-    lag = block_count - 1
+    lag = 1
     pending = None
     for now in range(CHUNKS + lag):
-        if now < CHUNKS + lag - 1:
+        if now < CHUNKS:
             forward(now)
         done = [g for g in GROUPS if g[0] + g[1] - 1 + lag == now]
         if not done:
@@ -258,18 +253,23 @@
         pltpu.make_async_copy(whole, whole, send_sem).wait()
 
     for section in range(SECTIONS):
-        source = lax.rem(r + section, block_count)
-        whole = left.at[section, half]
-
-        @pl.when(jnp.logical_and(has_prev, source >= place))
-        def _():
-            all_sent(whole, z_send.at[0, section])
-
-        @pl.when(jnp.logical_and(has_next, source <= place))
-        def _():
-            all_sent(whole, z_send.at[1, section])
-
-        all_sent(whole, y_send.at[section])
+        all_sent(left.at[section, half], y_send.at[section])
+
+    @pl.when(own_section < SECTIONS)
+    def _():
+        def step(distance, carry):
+            @pl.when(place >= distance)
+            def _():
+                all_sent(left.at[own_section, half], z_send.at[0, distance - 1])
+
+            @pl.when(place + distance < block_count)
+            def _():
+                all_sent(left.at[own_section, half], z_send.at[1, distance - 1])
+
+            return carry
+
+        lax.fori_loop(1, block_count, step, 0)
+
     for sems in (right_send, square_send):
         for k in range(2):
             all_sent(right.at[0], sems.at[k])
@@ -300,7 +300,7 @@
             pltpu.VMEM(tall, jnp.bfloat16),
             pltpu.VMEM((blk, half_cols), jnp.float32),
             dma((SECTIONS, 2, CHUNKS)),
-            dma((2, SECTIONS)),
+            dma((2, col_count // 2 - 1)),
             dma((SECTIONS,)),
             dma((2, CHUNKS)),
             dma((2,)),

time: 53.5 us -> 55.8 us (1.043)
  the two profiles are of different devices: /device:TPU:25 before, /device:TPU:1 now
where the time goes in v5:
time: 55.8 us; the launch traced here: 55.6 us
  Pallas kernels  53.1 us (95%)
  local copies, waits for them, and re-layouts  2.52 us (5%)
    pallas_call x1, Pallas kernels, per_device(): pl.pallas_call(functools.partial(kernel, row_count, col_count), out_shape...  53.1 us
    unnamed x5, local copies, waits for them, and re-layouts  2.52 us

profile of v5, /device:TPU:1, one launch (start us, length us, event | category | flops | bytes accessed | tf_op | source)
XLA Modules:
  0.0 55.6 jit_solution(11788751732875609874)
XLA Ops:
  0.0 0.0 copy-start.1
  0.0 0.7 %copy-done.1 = s32[4,2]{0,1:T(2,128)S(1)} copy-done((s32[4,2]{0,1:T(2,128)S(1)}, s32[4,2]{0,1:T(2,128)}, u32[]{:S(2)}) %copy-start.1) | copy-done | bytes 56
  0.7 0.0 copy-start
  0.7 1.0 %copy-done = f32[512,256]{1,0:T(8,128)S(1)} copy-done((f32[512,256]{1,0:T(8,128)S(1)}, f32[512,256]{1,0:T(8,128)}, u32[]{:S(2)}) %copy-start) | copy-done | bytes 524312
  1.7 53.1 %shard_map.28 = f32[512,256]{1,0:T(8,128)S(1)} custom-call(s32[2,4]{1,0:T(2,128)S(1)} %bitcast.1, f32[512,256]{1,0:T(8,128)S(1)} %copy-done), custom_call_target="tpu_custom_call" | custom-call | flops 2415919104 | bytes 1048576 | tf_op jit(solution)/shard_map/pallas_call | solution.py:285
  54.8 0.8 %copy.4 = f32[512,256]{1,0:T(8,128)} copy(f32[512,256]{1,0:T(8,128)S(1)} %shard_map.28) | data formatting | bytes 1048576
Async XLA Ops:
  0.0 0.7 %copy-start.1 = (s32[4,2]{0,1:T(2,128)S(1)}, s32[4,2]{0,1:T(2,128)}, u32[]{:S(2)}) copy-start(s32[4,2]{0,1:T(2,128)} %param.3) | copy-start | bytes 100
  0.7 1.0 %copy-start = (f32[512,256]{1,0:T(8,128)S(1)}, f32[512,256]{1,0:T(8,128)}, u32[]{:S(2)}) copy-start(f32[512,256]{1,0:T(8,128)} %den_ref.1) | copy-start | bytes 1572868

commit v6 on v3

--- a/solution.py
+++ b/solution.py
@@ -10,7 +10,7 @@
 SECTIONS = 3
 CHUNKS = 8
 GROUPS = ((0, 2), (2, 2), (4, 2), (6, 1), (7, 1))
-AHEAD = 2
+AHEAD = 4
 ROW_TILE = 128
 MESH = pl.DeviceIdType.MESH
 
@@ -226,10 +226,12 @@
         def step(tile, carry):
             span = pl.ds(pl.multiple_of(tile * ROW_TILE, ROW_TILE), ROW_TILE)
             total = cube[span, :] if last else jnp.zeros((ROW_TILE, half_cols), jnp.float32)
-            for section, side in terms:
-                depth = slice(side * half_cols, (side + 1) * half_cols)
+            for section, first, end in terms:
+                side = first // half_cols
+                depth = slice(first, end)
+                cols = slice(first - side * half_cols, end - side * half_cols)
                 total = total + product(
-                    left_high[section, side, span, :], left_low[section, side, span, :],
+                    left_high[section, side, span, cols], left_low[section, side, span, cols],
                     right_high[section, depth, :], right_low[section, depth, :],
                 )
             cube[span, :] = total
@@ -237,18 +239,22 @@
 
         lax.fori_loop(0, blk // ROW_TILE, step, 0)
 
+    late = blk - half_cols // 2
     split_right(square, 0, 0, blk)
-    for chunk in range(CHUNKS // 2):
+    for chunk in range(late // rows):
         wait_next(square, chunk, square_send, square_recv)
-    split_right(square, 1, 0, half_cols)
-    split_right(square, 2, 0, half_cols)
-    accumulate([(0, 0), (0, 1), (1, 0), (2, 0)], False)
+    split_right(square, 1, 0, late)
+    split_right(square, 2, 0, late)
+    early = [(0, 0, half_cols), (0, half_cols, blk)]
+    for section in range(1, SECTIONS):
+        early += [(section, 0, half_cols), (section, half_cols, late)]
+    accumulate(early, False)
     relay_right(square, CHUNKS - 1, square_send, square_recv)
-    split_right(square, 2, half_cols, half_cols)
-    for chunk in range(CHUNKS // 2, CHUNKS):
+    split_right(square, 2, late, blk - late)
+    for chunk in range(late // rows, CHUNKS):
         wait_next(square, chunk, square_send, square_recv)
-    split_right(square, 1, half_cols, half_cols)
-    accumulate([(1, 1), (2, 1)], True)
+    split_right(square, 1, late, blk - late)
+    accumulate([(section, late, blk) for section in range(1, SECTIONS)], True)
 
     for i in range(tile_rows):
         span = slice(i * tr, (i + 1) * tr)

time: 53.5 us -> 54.4 us (1.017)
  Pallas kernels: 50.8 us -> 51.7 us
    pallas_call x1, Pallas kernels: 50.8 us -> 51.7 us  [per_device(): pl.pallas_call(functools.partial(kernel, row_count, col_count), out_shape...]
where the time goes in v6:
time: 54.4 us; the launch traced here: 54.2 us
  Pallas kernels  51.7 us (95%)
  local copies, waits for them, and re-layouts  2.52 us (5%)
    pallas_call x1, Pallas kernels, per_device(): pl.pallas_call(functools.partial(kernel, row_count, col_count), out_shape...  51.7 us
    unnamed x5, local copies, waits for them, and re-layouts  2.52 us

profile of v6, /device:TPU:25, one launch (start us, length us, event | category | flops | bytes accessed | tf_op | source)
XLA Modules:
  0.0 54.2 jit_solution(8952501576785079650)
XLA Ops:
  0.0 0.0 copy-start.1
  0.0 0.7 %copy-done.1 = s32[4,2]{0,1:T(2,128)S(1)} copy-done((s32[4,2]{0,1:T(2,128)S(1)}, s32[4,2]{0,1:T(2,128)}, u32[]{:S(2)}) %copy-start.1) | copy-done | bytes 56
  0.7 0.0 copy-start
  0.7 1.0 %copy-done = f32[512,256]{1,0:T(8,128)S(1)} copy-done((f32[512,256]{1,0:T(8,128)S(1)}, f32[512,256]{1,0:T(8,128)}, u32[]{:S(2)}) %copy-start) | copy-done | bytes 524312
  1.7 51.7 %shard_map.28 = f32[512,256]{1,0:T(8,128)S(1)} custom-call(s32[2,4]{1,0:T(2,128)S(1)} %bitcast.1, f32[512,256]{1,0:T(8,128)S(1)} %copy-done), custom_call_target="tpu_custom_call" | custom-call | flops 2415919104 | bytes 1048576 | tf_op jit(solution)/shard_map/pallas_call | solution.py:291
  53.4 0.8 %copy.4 = f32[512,256]{1,0:T(8,128)} copy(f32[512,256]{1,0:T(8,128)S(1)} %shard_map.28) | data formatting | bytes 1048576
Async XLA Ops:
  0.0 0.7 %copy-start.1 = (s32[4,2]{0,1:T(2,128)S(1)}, s32[4,2]{0,1:T(2,128)}, u32[]{:S(2)}) copy-start(s32[4,2]{0,1:T(2,128)} %param.3) | copy-start | bytes 100
  0.7 1.0 %copy-start = (f32[512,256]{1,0:T(8,128)S(1)}, f32[512,256]{1,0:T(8,128)}, u32[]{:S(2)}) copy-start(f32[512,256]{1,0:T(8,128)} %den_ref.1) | copy-start | bytes 1572868

commit v7 on v3

--- a/solution.py
+++ b/solution.py
@@ -309,7 +309,7 @@
             dma,
         ],
         compiler_params=pltpu.CompilerParams(
-            collective_id=0, has_side_effects=True, vmem_limit_bytes=40 * 2**20
+            collective_id=0, has_side_effects=True, vmem_limit_bytes=53 * 2**20
         ),
         cost_estimate=pl.CostEstimate(
             flops=flops, bytes_accessed=2 * 4 * blk * half_cols, transcendentals=0

time: 53.5 us -> 52.4 us (0.979)
  local copies, waits for them, and re-layouts: 2.52 us -> 1.47 us
    unnamed x5 -> x3, local copies, waits for them, and re-layouts: 2.52 us -> 1.47 us
where the time goes in v7:
time: 52.4 us; the launch traced here: 52.2 us
  Pallas kernels  50.7 us (97%)
  local copies, waits for them, and re-layouts  1.47 us (3%)
    pallas_call x1, Pallas kernels, per_device(): pl.pallas_call(functools.partial(kernel, row_count, col_count), out_shape...  50.7 us
    unnamed x3, local copies, waits for them, and re-layouts  1.47 us

profile of v7, /device:TPU:25, one launch (start us, length us, event | category | flops | bytes accessed | tf_op | source)
XLA Modules:
  0.0 52.2 jit_solution(6825409769937887116)
XLA Ops:
  0.0 0.0 copy-start
  0.0 0.7 %copy-done = s32[4,2]{0,1:T(2,128)S(1)} copy-done((s32[4,2]{0,1:T(2,128)S(1)}, s32[4,2]{0,1:T(2,128)}, u32[]{:S(2)}) %copy-start) | copy-done | bytes 56
  0.7 50.7 %shard_map.28 = f32[512,256]{1,0:T(8,128)S(1)} custom-call(s32[2,4]{1,0:T(2,128)S(1)} %bitcast.1, f32[512,256]{1,0:T(8,128)} %den_ref.1), custom_call_target="tpu_custom_call" | custom-call | flops 2415919104 | bytes 1048576 | tf_op jit(solution)/shard_map/pallas_call | solution.py:285
  51.4 0.8 %copy.4 = f32[512,256]{1,0:T(8,128)} copy(f32[512,256]{1,0:T(8,128)S(1)} %shard_map.28) | data formatting | bytes 1048576
Async XLA Ops:
  0.0 0.7 %copy-start = (s32[4,2]{0,1:T(2,128)S(1)}, s32[4,2]{0,1:T(2,128)}, u32[]{:S(2)}) copy-start(s32[4,2]{0,1:T(2,128)} %param.3) | copy-start | bytes 100

commit v8 on v7

--- a/solution.py
+++ b/solution.py
@@ -130,7 +130,10 @@
         if now + AHEAD < CHUNKS:
             send_own(now + AHEAD)
 
-        def step(distance, carry):
+        nearest, furthest = max(1, now + 2 - CHUNKS), min(block_count - 1, now + 1)
+
+        def step(index, carry):
+            distance = nearest + furthest - index
             chunk = now + 1 - distance
             for sign in (-1, 1):
                 source = place + sign * distance
@@ -144,7 +147,7 @@
 
             return carry
 
-        lax.fori_loop(max(1, now + 2 - CHUNKS), min(block_count - 1, now + 1) + 1, step, 0)
+        lax.fori_loop(nearest, furthest + 1, step, 0)
 
     def right_copy(buffer, from_slot, to_slot, chunk, send_sem, recv_sems, device_row):
         span = pl.ds(chunk * rows, rows)

time: 52.4 us -> 51.2 us (0.977)
  the two profiles are of different devices: /device:TPU:25 before, /device:TPU:1 now
where the time goes in v8:
time: 51.2 us; the launch traced here: 51.1 us
  Pallas kernels  49.6 us (97%)
  local copies, waits for them, and re-layouts  1.47 us (3%)
    pallas_call x1, Pallas kernels, per_device(): pl.pallas_call(functools.partial(kernel, row_count, col_count), out_shape...  49.6 us
    unnamed x3, local copies, waits for them, and re-layouts  1.47 us

profile of v8, /device:TPU:1, one launch (start us, length us, event | category | flops | bytes accessed | tf_op | source)
XLA Modules:
  0.0 51.1 jit_solution(10939196646286433411)
XLA Ops:
  0.0 0.0 copy-start
  0.0 0.7 %copy-done = s32[4,2]{0,1:T(2,128)S(1)} copy-done((s32[4,2]{0,1:T(2,128)S(1)}, s32[4,2]{0,1:T(2,128)}, u32[]{:S(2)}) %copy-start) | copy-done | bytes 56
  0.7 49.6 %shard_map.28 = f32[512,256]{1,0:T(8,128)S(1)} custom-call(s32[2,4]{1,0:T(2,128)S(1)} %bitcast.1, f32[512,256]{1,0:T(8,128)} %den_ref.1), custom_call_target="tpu_custom_call" | custom-call | flops 2415919104 | bytes 1048576 | tf_op jit(solution)/shard_map/pallas_call | solution.py:288
  50.3 0.8 %copy.4 = f32[512,256]{1,0:T(8,128)} copy(f32[512,256]{1,0:T(8,128)S(1)} %shard_map.28) | data formatting | bytes 1048576
Async XLA Ops:
  0.0 0.7 %copy-start = (s32[4,2]{0,1:T(2,128)S(1)}, s32[4,2]{0,1:T(2,128)}, u32[]{:S(2)}) copy-start(s32[4,2]{0,1:T(2,128)} %param.3) | copy-start | bytes 100

commit v9 on v8

--- a/solution.py
+++ b/solution.py
@@ -127,9 +127,6 @@
             spread(own_section, chunk, True, True)
 
     def forward(now):
-        if now + AHEAD < CHUNKS:
-            send_own(now + AHEAD)
-
         nearest, furthest = max(1, now + 2 - CHUNKS), min(block_count - 1, now + 1)
 
         def step(index, carry):
@@ -148,6 +145,8 @@
             return carry
 
         lax.fori_loop(nearest, furthest + 1, step, 0)
+        if now + AHEAD < CHUNKS:
+            send_own(now + AHEAD)
 
     def right_copy(buffer, from_slot, to_slot, chunk, send_sem, recv_sems, device_row):
         span = pl.ds(chunk * rows, rows)

time: 51.2 us -> 50.9 us (level)
  no operation moved by 1% of the time
where the time goes in v9:
time: 50.9 us; the launch traced here: 50.8 us
  Pallas kernels  49.3 us (97%)
  local copies, waits for them, and re-layouts  1.47 us (3%)
    pallas_call x1, Pallas kernels, per_device(): pl.pallas_call(functools.partial(kernel, row_count, col_count), out_shape...  49.3 us
    unnamed x3, local copies, waits for them, and re-layouts  1.47 us

profile of v9, /device:TPU:1, one launch (start us, length us, event | category | flops | bytes accessed | tf_op | source)
XLA Modules:
  0.0 50.8 jit_solution(14362472871640465619)
XLA Ops:
  0.0 0.0 copy-start
  0.0 0.7 %copy-done = s32[4,2]{0,1:T(2,128)S(1)} copy-done((s32[4,2]{0,1:T(2,128)S(1)}, s32[4,2]{0,1:T(2,128)}, u32[]{:S(2)}) %copy-start) | copy-done | bytes 56
  0.7 49.3 %shard_map.28 = f32[512,256]{1,0:T(8,128)S(1)} custom-call(s32[2,4]{1,0:T(2,128)S(1)} %bitcast.1, f32[512,256]{1,0:T(8,128)} %den_ref.1), custom_call_target="tpu_custom_call" | custom-call | flops 2415919104 | bytes 1048576 | tf_op jit(solution)/shard_map/pallas_call | solution.py:287
  50.0 0.8 %copy.4 = f32[512,256]{1,0:T(8,128)} copy(f32[512,256]{1,0:T(8,128)S(1)} %shard_map.28) | data formatting | bytes 1048576
Async XLA Ops:
  0.0 0.7 %copy-start = (s32[4,2]{0,1:T(2,128)S(1)}, s32[4,2]{0,1:T(2,128)}, u32[]{:S(2)}) copy-start(s32[4,2]{0,1:T(2,128)} %param.3) | copy-start | bytes 100
